TPU v7x, 256 devices: a whole 4x4x8 slice. The times are simulated.
256 devices in a mesh: inner: 32 (over z, y), outer: 4 (over x_hi, core), head: 2 (over x_lo).
Axes of the slice: x: 4 (x_hi: 2, x_lo: 2; x = x_hi * 2 + x_lo), y: 4, z: 8, core: 2. Of those that a mesh axis runs over, the one named last changes fastest.
Arguments:
- queries: bfloat16 [2, 49152, 2, 4, 128], P(None, ('inner', 'outer'), 'head'), may hold values from -5 to 5
- grad_out: bfloat16 [2, 49152, 2, 4, 128], P(None, ('inner', 'outer'), 'head'), may hold values from -6 to 6
- keys_values: bfloat16 [49152, 2, 2, 128], P(('inner', 'outer'), 'head'), may hold values from -5 to 5
- inputs: bfloat16 [49152, 4096], P(('inner', 'outer')), may hold values from -24 to 24
- kv_weight: bfloat16 [4096, 2, 2, 128], P(None, 'head'), may hold values from -0.09375 to 0.09375
- block_order: int32 [128], replicated, may hold values from 0 to 127, each once
Outputs:
- query_grads: bfloat16 [2, 49152, 2, 4, 128], P(None, ('inner', 'outer'), 'head')
- input_grads: bfloat16 [49152, 4096], P(('inner', 'outer'), 'head')
- weight_grads: float32 [4096, 2, 2, 128], P(('inner', 'outer'), 'head')
Inputs may be any that keep to these rules, and one draw needn't show every extreme that they name: `block_order`: each value appears exactly once.
All inputs are finite; a program needn't handle non-finite values.
Results may differ from a plain program's by a relative error of at most 0.015.
Values may be sent and summed in bfloat16 or wider, within the bound.
A program may use at most 128 MiB of HBM per device.

v0:
```python
import math

import jax
import jax.numpy as jnp
from jax import lax
from jax.sharding import PartitionSpec as P

STEPS = 3


def passed_along(array, axis, by):
    count = lax.axis_size(axis)
    return lax.ppermute(array, axis, [(i, (i + by) % count) for i in range(count)])


def block_scores(query_rows, grad_rows, key_block, visible_mask, score_scale):
    keys_only = key_block[:, 0]
    values_only = key_block[:, 1]
    logits = (
        jnp.einsum("lthd,sd->lhts", query_rows, keys_only, preferred_element_type=jnp.float32)
        * score_scale
    )
    logits = jnp.where(visible_mask, logits, -jnp.inf)
    grad_probs = jnp.einsum(
        "lthd,sd->lhts", grad_rows, values_only, preferred_element_type=jnp.float32
    )
    return (logits, grad_probs)


def absorb(running, logits, grad_probs):
    run_max, run_total, run_dot = running
    new_max = jnp.maximum(run_max, jnp.max(logits, axis=-1))
    factor = jnp.exp(run_max - new_max)
    weights = jnp.exp(logits - new_max[..., None])
    new_total = run_total * factor + jnp.sum(weights, axis=-1)
    new_dot = run_dot * factor + jnp.sum(weights * grad_probs, axis=-1)
    return (new_max, new_total, new_dot)


def backward_terms(
    query_rows, grad_rows, key_block, visible_mask, score_scale, log_total, delta_rows
):
    logits, grad_probs = block_scores(query_rows, grad_rows, key_block, visible_mask, score_scale)
    probs_full = jnp.exp(logits - log_total[..., None])
    grad_logits = (probs_full * (grad_probs - delta_rows[..., None]) * score_scale).astype(
        jnp.bfloat16
    )
    probs_low = probs_full.astype(jnp.bfloat16)
    query_grad = jnp.einsum(
        "lhts,sd->lthd", grad_logits, key_block[:, 0], preferred_element_type=jnp.float32
    )
    key_grad = jnp.einsum(
        "lhts,lthd->sd", grad_logits, query_rows, preferred_element_type=jnp.float32
    )
    value_grad = jnp.einsum(
        "lhts,lthd->sd", probs_low, grad_rows, preferred_element_type=jnp.float32
    )
    return (query_grad, jnp.stack([key_grad, value_grad], axis=1))


def attend(query_rows, grad_rows, key_blocks, block_masks, score_scale):
    shape_rows = (query_rows.shape[0], query_rows.shape[2], query_rows.shape[1])
    zero_stats = jnp.zeros(shape_rows, jnp.float32)
    running = (jnp.full(shape_rows, -jnp.inf, jnp.float32), zero_stats, zero_stats)
    for number in range(len(key_blocks)):
        logits, grad_probs = block_scores(
            query_rows, grad_rows, key_blocks[number], block_masks[number], score_scale
        )
        running = absorb(running, logits, grad_probs)
    log_total = running[0] + jnp.log(running[1])
    delta_rows = running[2] / running[1]
    query_grad = jnp.zeros(query_rows.shape, jnp.float32)
    partials = []
    for number in range(len(key_blocks)):
        step_query, step_pairs = backward_terms(
            query_rows,
            grad_rows,
            key_blocks[number],
            block_masks[number],
            score_scale,
            log_total,
            delta_rows,
        )
        query_grad = query_grad + step_query
        partials.append(step_pairs)
    return (query_grad, partials)


def shards(queries, grad_out, keys_values, inputs, kv_weight, block_order):
    rows_dev = queries.shape[1]
    head_size = queries.shape[4]
    width = inputs.shape[1]
    score_scale = 1.0 / math.sqrt(head_size)
    inner_count = lax.axis_size("inner")
    outer_count = lax.axis_size("outer")
    inner_index = lax.axis_index("inner")
    outer_index = lax.axis_index("outer")
    positions = jnp.arange(rows_dev, dtype=jnp.int32)
    block_slots = jnp.arange(block_order.shape[0], dtype=jnp.int32)

    def place_of(block_id):
        return jnp.sum(jnp.where(block_slots == block_id, block_order, 0))

    my_place = place_of(inner_index * outer_count + outer_index)
    query_pos = my_place * rows_dev + positions
    block_ids = [
        (inner_index - distance) % inner_count * outer_count + outer_index
        for distance in range(STEPS)
    ]
    block_ids.append(inner_index * outer_count + (outer_index - 1) % outer_count)
    places = [place_of(block_id) for block_id in block_ids]
    block_masks = [
        (place * rows_dev + positions)[None, :] <= query_pos[:, None] for place in places
    ]
    keys_local = keys_values[:, 0]
    query_rows = queries[:, :, 0]
    grad_rows = grad_out[:, :, 0]
    grad_parts = []
    pair_grads = jnp.zeros(keys_local.shape, jnp.float32)
    for layer_index in range(query_rows.shape[0]):
        one_query_rows = query_rows[layer_index : layer_index + 1]
        one_grad_rows = grad_rows[layer_index : layer_index + 1]
        key_blocks = [keys_local]
        moving = keys_local
        for one_distance in range(1, STEPS):
            moving = passed_along(moving, "inner", 1)
            key_blocks.append(moving)
        key_blocks.append(passed_along(keys_local, "outer", 1))
        one_query_grad, partials = attend(
            one_query_rows, one_grad_rows, key_blocks, block_masks, score_scale
        )
        carried = partials[STEPS - 1]
        for one_distance in range(STEPS - 2, -1, -1):
            carried = (
                passed_along(carried.astype(jnp.bfloat16), "inner", -1).astype(carried.dtype)
                + partials[one_distance]
            )
        carried = carried + passed_along(partials[STEPS].astype(jnp.bfloat16), "outer", -1).astype(
            jnp.float32
        )
        grad_parts.append(one_query_grad)
        pair_grads = pair_grads + carried
    query_grad = jnp.concatenate(grad_parts, axis=0)
    query_out = query_grad.astype(jnp.bfloat16)[:, :, None]
    pairs_low = pair_grads.astype(jnp.bfloat16)
    grads_flat = pairs_low.reshape(rows_dev, 2 * head_size)
    weight_flat = kv_weight[:, 0].reshape(width, 2 * head_size)
    input_term = lax.dot_general(
        grads_flat, weight_flat, (((1,), (1,)), ((), ())), preferred_element_type=jnp.float32
    )
    input_grad = lax.psum_scatter(
        input_term.astype(jnp.bfloat16), "head", scatter_dimension=1, tiled=True
    )
    token_count = rows_dev * inner_count * outer_count
    product = lax.dot_general(
        inputs, grads_flat, (((0,), (0,)), ((), ())), preferred_element_type=jnp.float32
    )
    weight_sum = lax.psum_scatter(
        product.reshape(
            width // (inner_count * outer_count) * lax.axis_size(("inner", "outer")),
            1,
            2,
            head_size,
        ),
        ("inner", "outer"),
        scatter_dimension=0,
        tiled=True,
    )
    weight_grad = weight_sum / math.sqrt(token_count)
    return (query_out, input_grad, weight_grad)


def solution(mesh):
    return jax.shard_map(
        shards,
        mesh=mesh,
        in_specs=(
            P(None, ("inner", "outer"), "head", None, None),
            P(None, ("inner", "outer"), "head", None, None),
            P(("inner", "outer"), "head", None, None),
            P(("inner", "outer"), None),
            P(None, "head", None, None),
            P(),
        ),
        out_specs=(
            P(None, ("inner", "outer"), "head", None, None),
            P(("inner", "outer"), "head"),
            P(("inner", "outer"), "head", None, None),
        ),
        check_vma=False,
    )
```

profile of v0, /device:TPU:1, one launch (start us, length us, event | category | flops | bytes accessed | tf_op | source)
XLA Modules:
  0.0 1418.3 jit_solution(9817134505721368050)
XLA Ops:
  8.1 1.1 copy.194
  9.2 2.2 collective-permute-start
  11.4 3.6 collective-permute-start.2
  15.0 1.4 fusion.173
  19.6 1.4 fusion.177
  21.0 1.4 fusion.178
  22.8 0.5 fusion.185
  23.3 0.5 fusion.181
  23.9 0.6 fusion.28
  24.5 0.6 fusion.12
  25.1 1.4 fusion.183
  26.6 1.4 fusion.179
  28.0 1.6 collective-permute-start.1
  29.6 0.5 fusion.186
  30.1 0.5 fusion.182
  30.7 7.2 collective-permute-done.1
  37.9 0.5 fusion.184
  38.4 2.0 fusion.20
  40.4 2.0 fusion.24
  42.4 2.9 fusion.16
  45.3 1.1 fusion.140
  46.4 1.2 fusion.99
  47.6 1.1 fusion.143
  48.8 0.5 fusion.180
  49.3 2.0 fusion.8
  51.3 3.4 fusion
  54.8 2.6 fusion.4
  57.4 0.6 log_add_fusion
  58.0 0.5 fusion.146
  58.5 1.2 fusion.111
  59.7 0.5 fusion.149
  60.3 0.5 fusion.96
  60.8 0.5 fusion.108
  61.3 0.6 add_divide_fusion.1
  61.9 5.2 fusion.82
  67.7 2.5 pad_maximum_fusion.1
  70.2 2.0 collective-permute-start.3
  73.3 3.5 fusion.86
  76.9 0.5 fusion.137
  77.4 1.5 collective-permute-start.6
  79.4 0.5 fusion.136
  80.0 3.1 collective-permute-start.8
  83.6 0.5 collective-permute-start.4
  84.2 2.7 collective-permute-start.7
  87.4 2.0 collective-permute-done.4
  89.4 4.2 collective-permute-done.7
  93.6 0.8 fusion.155
  94.5 1.8 copy.89
  96.2 4.1 fusion.187
  100.3 7.2 copy.90
  107.8 4.4 convolution_convert_fusion
  112.3 0.6 copy-done.25
  112.9 0.6 dynamic-slice
  114.2 1.9 fusion.167
  116.1 1.9 fusion.169
  118.0 0.5 convolution_add_fusion.3
  118.5 0.5 fusion.55
  119.2 0.5 fusion.166
  119.9 1.5 fusion.168
  121.4 0.5 convolution_add_fusion.1
  121.9 0.5 fusion.54
  122.5 1.5 copy.91
  124.0 1285.5 %all-reduce.3.cloned.1.call-done = f32[4096,1,2,128]{3,2,1,0:T(2,128)} async-done(((f32[4096,1,2,128]{3,2,1,0:T(2,128)}), f32[4096,1,2,128]{3,2,1,0:T(2,128)}) %all-reduce.3.cloned.1.call-update) | async-done | bytes 4194320
  1409.5 1.4 dynamic-slice_multiply_fusion
  (83 shorter events, 4.4 us)
Async XLA Ops:
  8.0 88.2 %copy-start = (bf16[384,4096]{1,0:T(8,128)(2,1)S(1)}, bf16[384,4096]{1,0:T(8,128)(2,1)}, u32[]{:S(2)}) copy-start(bf16[384,4096]{1,0:T(8,128)(2,1)} %param.9) | copy-start | bytes 9437188
  8.0 1401.5 %all-reduce.3.cloned.1.call-start = ((), (), s32[]{:S(2)}) async-start(), calls=%async_computation.2 | async-start | bytes 8388608
  9.2 18.9 %collective-permute-start = (bf16[384,2,128]{2,0,1:T(8,128)(2,1)S(1)}, bf16[384,2,128]{2,0,1:T(8,128)(2,1)S(1)}, u32[]{:S(2)}, u32[]{:S(2)}) collective-permute-start(bf16[384,2,128]{2,0,1:T(8,128)(2,1)S(1)} %bitcast.513), channel_id=1, source_target_pairs={{0,8},{8,16},{16,24},{24,32},{32,40},{40,48},{48,56},{56,64},{64,7... | collective-permute-start | bytes 589832 | tf_op jit(solution)/shard_map/ppermute | solution.py:13
  11.4 13.8 collective-permute-start.2
  28.0 9.9 collective-permute-start.1
  37.9 16.9 %copy-start.17 = (bf16[384,2,128]{2,0,1:T(8,128)(2,1)}, bf16[384,2,128]{2,0,1:T(8,128)(2,1)S(1)}, u32[]{:S(2)}) copy-start(bf16[384,2,128]{2,0,1:T(8,128)(2,1)S(1)} %collective-permute-done.1) | copy-start | bytes 589828
  67.1 6.0 copy-start.4
  67.1 6.0 copy-start.10
  67.1 15.9 %copy-start.1 = (bf16[4,384,384]{1,2,0:T(8,128)(2,1)}, bf16[4,384,384]{1,2,0:T(8,128)(2,1)S(1)}, u32[]{:S(2)}) copy-start(bf16[4,384,384]{1,2,0:T(8,128)(2,1)S(1)} %get-tuple-element.50) | copy-start | bytes 3538948
  67.1 5.5 copy-start.14
  67.1 6.0 copy-start.21
  67.2 6.2 copy-start.9
  67.6 5.6 copy-start.22
  67.7 5.6 copy-start.23
  67.7 5.6 copy-start.24
  67.7 5.7 copy-start.8
  70.2 13.3 collective-permute-start.3
  73.2 14.2 %collective-permute-start.5 = (bf16[384,2,128]{2,0,1:T(8,128)(2,1)S(1)}, bf16[384,2,128]{2,0,1:T(8,128)(2,1)S(1)}, u32[]{:S(2)}, u32[]{:S(2)}) collective-permute-start(bf16[384,2,128]{2,0,1:T(8,128)(2,1)S(1)} %pad_maximum_fusion.2), channel_id=1, source_target_pairs={{0,6},{2,0},{4,2},{6,4},{1,7},{3,1},{5,3},{7,5},{8,14},{10,8},{12,... | collective-permute-start | bytes 589832 | tf_op jit(solution)/shard_map/ppermute | solution.py:13
  76.9 3.1 copy-start.6
  76.9 3.1 copy-start.12
  76.9 3.1 copy-start.15
  76.9 10.0 copy-start.2
  77.4 6.7 collective-permute-start.6
  79.4 4.1 copy-start.19
  79.4 4.7 copy-start.20
  80.0 7.4 collective-permute-start.8
  83.6 5.9 collective-permute-start.4
  84.2 9.5 collective-permute-start.7
  107.5 1303.3 %reduce-scatter.2.cloned.1.call-start = ((), (), s32[]{:S(2)}) async-start(), calls=%async_computation.1 | async-start | bytes 4718592 | tf_op jit(solution)/shard_map/reduce_scatter | solution.py:151
  112.2 0.7 copy-start.25
  114.1 3.8 copy-start.5
  116.0 2.5 copy-start.11
  116.0 2.5 copy-start.18
  118.0 1.3 copy-start.3
  118.5 1.4 copy-start.16
  119.2 2.1 copy-start.7
  119.9 2.0 copy-start.13
Sparse Core Ops, SparseCore 0:
  107.7 1301.7 all-reduce.2
Sparse Core Ops, SparseCore 1:
  112.3 47.9 reduce-scatter.1
where the time goes:
time: 1420 us
  waiting for transfers between devices  1300 us (92%)
  matrix products  49 us (3%)
  between operations  20 us (1%)
  starting transfers between devices  17.6 us (1%)
  other arithmetic  16.7 us (1%)
  local copies, waits for them, and re-layouts  16 us (1%)
    unnamed x3, waiting for transfers between devices  1290 us
  transfers between devices with their start and end apart: 11, of which 4 were waited for; matrix products, arithmetic and copies ran while one was open for 2% of the time, Pallas kernels for 0%

commit v1 on v0

v1 whole, which is shorter than its diff:
```python
import functools
import math

import jax
import jax.numpy as jnp
from jax import lax
from jax.experimental import pallas as pl
from jax.experimental.pallas import tpu as pltpu
from jax.sharding import PartitionSpec as P

F32 = jnp.float32
BF16 = jnp.bfloat16
MESH = pl.DeviceIdType.MESH
N_INNER = 32
N_Y = 4
N_Z = 8
N_OUTER = 4
NT = (((1,), (1,)), ((), ()))
TN = (((0,), (0,)), ((), ()))
NN = (((1,), (0,)), ((), ()))
FAR = -1e30
TILE = 512


def dot(a, b, dims):
    return lax.dot_general(a, b, dims, preferred_element_type=F32)


def remote(src, dst, send, recv, **where):
    return pltpu.make_async_remote_copy(
        src_ref=src,
        dst_ref=dst,
        send_sem=send,
        recv_sem=recv,
        device_id=where,
        device_id_type=MESH,
    )


def kernel(
    q, go, kv_raw, order, inputs, weight,
    dq, ig, wg,
    S, DP, top, total, delta, dqt, kv, gout, gin, inp, w_own, w_oth, w_cat,
    pair, pair_t, prod, near, ysend, yfar, relay, yrecv, yacc, zsend, zrecv, fsend, frecv,
    kv_ss, kv_rs, g_ss, g_rs, in_ls, in_ss, in_rs, w_ls, w_ss, w_rs, p_ss, p_rs,
    far_ss, far_rs, y_ss, y_rs, z_ss, z_rs, f_ss, f_rs,
):
    rows = q.shape[0]
    tok = kv.shape[2]
    hd = kv.shape[3]
    group = rows // 2 // tok
    scale = 1.0 / math.sqrt(hd)
    scale2 = scale * math.log2(math.e)
    half_w = w_own.shape[0]
    half_d = half_w // 2
    i = lax.axis_index("inner")
    o = lax.axis_index("outer")
    h = lax.axis_index("head")
    z = i // N_Y
    y = lax.rem(i, N_Y)
    xh = o // 2
    c = lax.rem(o, 2)

    def inner(by):
        return lax.rem(i + by + N_INNER, N_INNER)

    def outer(by):
        return lax.rem(o + by + N_OUTER, N_OUTER)

    def at_z(by):
        return lax.rem(z + by, N_Z) * N_Y + y

    def at_y(place):
        return z * N_Y + place

    core_mate = o + 1 - 2 * c

    barrier = pltpu.get_barrier_semaphore()
    greeted = [{"inner": inner(by)} for by in (1, 2, -1, -2)]
    greeted += [{"outer": outer(by)} for by in (1, 2, 3)]
    greeted += [{"head": 1 - h}]
    greeted += [{"inner": at_y(lax.rem(y + by, N_Y))} for by in (1, 3)]
    greeted += [{"inner": at_z(by)} for by in range(1, N_Z)]
    for where in greeted:
        pl.semaphore_signal(barrier, inc=1, device_id=where, device_id_type=MESH)

    kv[0, 0] = kv_raw[pl.ds(0, tok, 2), :]
    kv[0, 1] = kv_raw[pl.ds(1, tok, 2), :]
    w_local = pltpu.make_async_copy(
        weight.at[pl.ds(pl.multiple_of(h * half_w, half_w), half_w), :], w_own, w_ls
    )
    w_local.start()

    def in_local(zz):
        return pltpu.make_async_copy(
            inputs.at[:, pl.ds(pl.multiple_of(zz * 512 + c * 256, 256), 256)],
            inp.at[zz, pl.ds(0, tok), :],
            in_ls.at[zz],
        )

    def in_remote(zz):
        return remote(
            inputs.at[:, pl.ds(pl.multiple_of(zz * 512 + (1 - c) * 256, 256), 256)],
            inp.at[zz, pl.ds(tok, tok), :],
            in_ss.at[zz],
            in_rs.at[zz],
            outer=core_mate,
        )

    for zz in range(N_Z):
        in_local(zz).start()
    pl.semaphore_wait(barrier, len(greeted))

    forward = [
        remote(kv.at[0], kv.at[1], kv_ss.at[0], kv_rs.at[0], inner=inner(1)),
        remote(kv.at[0], kv.at[2], kv_ss.at[1], kv_rs.at[1], inner=inner(2)),
        remote(kv.at[0], kv.at[3], kv_ss.at[2], kv_rs.at[2], outer=outer(1)),
    ]
    back = [
        remote(gout.at[0], gin.at[0], g_ss.at[0], g_rs.at[0], inner=inner(-1)),
        remote(gout.at[1], gin.at[1], g_ss.at[1], g_rs.at[1], inner=inner(-2)),
        remote(gout.at[2], gin.at[2], g_ss.at[2], g_rs.at[2], outer=outer(-1)),
    ]
    for copy in forward:
        copy.start()
    w_remote = remote(
        weight.at[pl.ds(pl.multiple_of((1 - h) * half_w, half_w), half_w), :],
        w_oth,
        w_ss,
        w_rs,
        head=1 - h,
    )
    w_remote.start()
    for zz in range(N_Z):
        in_remote(zz).start()

    mine = order[i * N_OUTER + o]
    block_ids = [None, inner(-1) * N_OUTER + o, inner(-2) * N_OUTER + o, i * N_OUTER + outer(-1)]
    bias = [jnp.float32(0.0)]
    for block_id in block_ids[1:]:
        bias.append(jnp.where(order[block_id] < mine, 0.0, FAR).astype(F32))

    steps = rows // TILE

    def tile(t):
        return pl.ds(pl.multiple_of(t * TILE, TILE), TILE)

    def look(b):
        def body(t, carry):
            cs = tile(t)
            s = dot(kv[b, 0], q[cs, :], NT)
            if b == 0:
                key = lax.broadcasted_iota(jnp.int32, (tok, TILE), 0)
                row = lax.broadcasted_iota(jnp.int32, (tok, TILE), 1)
                token = (row + lax.rem(t * TILE, rows // 2)) // group
                s = jnp.where(key <= token, s, FAR)
            dp = dot(kv[b, 1], go[cs, :], NT)
            S[b, :, cs] = s
            DP[b, :, cs] = dp
            here = jnp.max(s, axis=0, keepdims=True) * scale2 + bias[b]
            if b == 0:
                e = jnp.exp2(s * scale2 - here)
                top[:, cs] = here
                total[:, cs] = jnp.sum(e, axis=0, keepdims=True)
                delta[:, cs] = jnp.sum(e * dp, axis=0, keepdims=True)
            else:
                old = top[:, cs]
                new = jnp.maximum(old, here)
                factor = jnp.exp2(old - new)
                e = jnp.exp2(s * scale2 - (new - bias[b]))
                top[:, cs] = new
                total[:, cs] = total[:, cs] * factor + jnp.sum(e, axis=0, keepdims=True)
                delta[:, cs] = delta[:, cs] * factor + jnp.sum(e * dp, axis=0, keepdims=True)
            return carry

        lax.fori_loop(0, steps, body, 0, unroll=2)

    def grads(b, first):
        def body(t, carry):
            dk, dv = carry
            cs = tile(t)
            p = jnp.exp2(S[b, :, cs] * scale2 - (top[:, cs] - bias[b]))
            ds = (p * (DP[b, :, cs] - delta[:, cs])).astype(BF16)
            part = dot(kv[b, 0], ds, TN)
            if first:
                dqt[:, cs] = part
            else:
                dqt[:, cs] += part
            return dk + dot(ds, q[cs, :], NN), dv + dot(p.astype(BF16), go[cs, :], NN)

        zero = jnp.zeros((tok, hd), F32)
        return lax.fori_loop(0, steps, body, (zero, zero), unroll=2)

    look(0)
    w_local.wait()
    w_cat[0, :, :hd] = w_own[pl.ds(0, half_d, 2), :]
    w_cat[0, :, hd:] = w_own[pl.ds(1, half_d, 2), :]
    for b in (1, 3, 2):
        forward[b - 1].wait_recv()
        look(b)
    sums = total[...]
    delta[...] = delta[...] / sums
    top[...] = top[...] + jnp.log2(sums)

    for number, b in enumerate((2, 1, 3)):
        dk, dv = grads(b, number == 0)
        gout[b - 1, :, :hd] = (dk * scale).astype(BF16)
        gout[b - 1, :, hd:] = dv.astype(BF16)
        back[b - 1].start()
    dk, dv = grads(0, False)
    dk = dk * scale
    for b in (2, 1, 3):
        back[b - 1].wait_recv()
        dk = dk + gin[b - 1, :, :hd].astype(F32)
        dv = dv + gin[b - 1, :, hd:].astype(F32)
    pair[0, :, :hd] = dk.astype(BF16)
    pair[0, :, hd:] = dv.astype(BF16)
    to_core = remote(pair.at[0], pair.at[1], p_ss.at[0], p_rs.at[0], outer=core_mate)
    to_head = remote(pair.at[0], pair.at[2], p_ss.at[1], p_rs.at[1], head=1 - h)
    to_core.start()
    to_head.start()
    pair_t[:hd, :tok] = dk.T.astype(BF16)
    pair_t[hd:, :tok] = dv.T.astype(BF16)
    to_core.wait_recv()
    pair_t[:, tok:] = pair[1].astype(F32).T.astype(BF16)
    for zz in range(N_Z):
        in_local(zz).wait()
        in_remote(zz).wait_recv()

    j_own = lax.rem(y, 2)
    j_near = 1 - j_own
    owner = y // 2 == c
    not_owner = y // 2 != c
    y_near = 2 * c + j_near
    from_above = lax.rem(y - y_near + N_Y, N_Y) == 1
    side = jnp.where(from_above, 0, 1)

    def z_at(zz):
        return lax.rem(z + 1 + zz, N_Z)

    def relays(zz):
        return (lax.rem(z_at(zz), 2) == 0) == from_above

    def far_copy(zz):
        by = jnp.where(lax.rem(z_at(zz), 2) == 0, N_Y - 1, 1)
        return remote(
            yfar.at[zz], relay.at[zz], far_ss.at[zz], far_rs.at[zz],
            inner=at_y(lax.rem(y + by, N_Y)),
        )

    def near_copy(zz):
        return remote(
            ysend.at[zz], yrecv.at[side, zz], y_ss.at[zz], y_rs.at[side, zz],
            inner=at_y(y_near),
        )

    def z_copy(zz):
        return remote(
            zsend.at[zz], zrecv.at[zz], z_ss.at[zz], z_rs.at[zz], inner=z_at(zz) * N_Y + y
        )

    def produce(zz, carry):
        x = dot(pair_t[...], inp[z_at(zz)], NN)
        prod[0] = x[:, :hd]
        prod[1] = x[:, hd:]

        @pl.when(owner)
        def _():
            yacc[zz] = prod[j_own]

        @pl.when(not_owner)
        def _():
            yfar[zz] = prod[j_own].astype(BF16)
            far_copy(zz).start()

        @pl.when(relays(zz))
        def _():
            near[zz] = prod[j_near]

        @pl.when(jnp.logical_not(relays(zz)))
        def _():
            ysend[zz] = prod[j_near].astype(BF16)
            near_copy(zz).start()

        return carry

    lax.fori_loop(0, N_Z, produce, 0)

    def pass_on(zz, carry):
        @pl.when(relays(zz))
        def _():
            far_copy(zz).wait_recv()
            ysend[zz] = (near[zz] + relay[zz].astype(F32)).astype(BF16)
            near_copy(zz).start()

        return carry

    lax.fori_loop(0, N_Z, pass_on, 0)

    def finish_queries(t, carry):
        cs = tile(t)
        dq[cs, :] = (dqt[:, cs] * scale).T.astype(BF16)
        return carry

    lax.fori_loop(0, steps, finish_queries, 0)
    w_remote.wait_recv()
    w_cat[1, :, :hd] = w_oth[pl.ds(0, half_d, 2), :]
    w_cat[1, :, hd:] = w_oth[pl.ds(1, half_d, 2), :]
    to_head.wait_recv()

    def input_part(t, carry):
        cs = tile(t)
        term = dot(pair[0], w_cat[0, cs, :], NT) + dot(pair[2], w_cat[1, cs, :], NT)
        ig[:, cs] = term.astype(BF16)
        return carry

    lax.fori_loop(0, half_d // TILE, input_part, 0)

    def fin_copy(by):
        place = (core_mate, lax.rem(o + 2, N_OUTER), N_OUTER - 1 - o)[by - 1]
        slot = 0 if by == 1 else 1
        return remote(
            fsend.at[place], frecv.at[slot], f_ss.at[by - 1], f_rs.at[slot], outer=place
        )

    @pl.when(owner)
    def _():
        def gather_y(zz, carry):
            for s in range(2):
                remote(
                    ysend.at[zz], yrecv.at[s, zz], y_ss.at[zz], y_rs.at[s, zz], inner=at_y(y_near)
                ).wait_recv()
            x = yacc[zz] + yrecv[0, zz].astype(F32) + yrecv[1, zz].astype(F32)
            yacc[zz] = x

            @pl.when(zz < N_Z - 1)
            def _():
                zsend[zz] = x.astype(BF16)
                z_copy(zz).start()

            return carry

        lax.fori_loop(0, N_Z, gather_y, 0)

        def gather_z(zz, x):
            z_copy(zz).wait_recv()
            return x + zrecv[zz].astype(F32)

        x = lax.fori_loop(0, N_Z - 1, gather_z, yacc[N_Z - 1])
        x = x.T / math.sqrt(tok * N_INNER * N_OUTER)
        for place in range(N_OUTER):
            fsend[place] = x[place * 32 : place * 32 + 32, :]
        for by in (3, 2, 1):
            fin_copy(by).start()

    @pl.when(owner)
    def _():
        fin_copy(2).wait_recv()
        x = fsend[o] + frecv[1]
        wg[pl.ds(0, 32, 2), :] = x[:, :hd]
        wg[pl.ds(1, 32, 2), :] = x[:, hd:]

    @pl.when(not_owner)
    def _():
        fin_copy(1).wait_recv()
        fin_copy(3).wait_recv()
        x = frecv[0] + frecv[1]
        wg[pl.ds(0, 32, 2), :] = x[:, :hd]
        wg[pl.ds(1, 32, 2), :] = x[:, hd:]

    for copy in forward + back + [w_remote, to_core, to_head]:
        copy.wait_send()

    def sent(zz, carry):
        in_remote(zz).wait_send()
        near_copy(zz).wait_send()

        @pl.when(not_owner)
        def _():
            far_copy(zz).wait_send()

        return carry

    lax.fori_loop(0, N_Z, sent, 0)

    @pl.when(owner)
    def _():
        for zz in range(N_Z - 1):
            z_copy(zz).wait_send()
        for by in (1, 2, 3):
            fin_copy(by).wait_send()


def shards(queries, grad_out, keys_values, inputs, kv_weight, block_order):
    layers, tok, _, per_group, hd = queries.shape
    rows = layers * tok * per_group
    width = inputs.shape[1]
    vmem = pl.BlockSpec(memory_space=pltpu.VMEM)
    smem = pl.BlockSpec(memory_space=pltpu.SMEM)
    hbm = pl.BlockSpec(memory_space=pl.ANY)
    dma = pltpu.SemaphoreType.DMA
    scratch = [
        pltpu.VMEM((4, tok, rows), F32),
        pltpu.VMEM((4, tok, rows), F32),
        pltpu.VMEM((1, rows), F32),
        pltpu.VMEM((1, rows), F32),
        pltpu.VMEM((1, rows), F32),
        pltpu.VMEM((hd, rows), F32),
        pltpu.VMEM((4, 2, tok, hd), BF16),
        pltpu.VMEM((3, tok, 2 * hd), BF16),
        pltpu.VMEM((3, tok, 2 * hd), BF16),
        pltpu.VMEM((N_Z, 2 * tok, 256), BF16),
        pltpu.VMEM((width, hd), BF16),
        pltpu.VMEM((width, hd), BF16),
        pltpu.VMEM((2, width // 2, 2 * hd), BF16),
        pltpu.VMEM((3, tok, 2 * hd), BF16),
        pltpu.VMEM((2 * hd, 2 * tok), BF16),
        pltpu.VMEM((2, 2 * hd, 128), F32),
        pltpu.VMEM((N_Z, 2 * hd, 128), F32),
        pltpu.VMEM((N_Z, 2 * hd, 128), BF16),
        pltpu.VMEM((N_Z, 2 * hd, 128), BF16),
        pltpu.VMEM((N_Z, 2 * hd, 128), BF16),
        pltpu.VMEM((2, N_Z, 2 * hd, 128), BF16),
        pltpu.VMEM((N_Z, 2 * hd, 128), F32),
        pltpu.VMEM((N_Z - 1, 2 * hd, 128), BF16),
        pltpu.VMEM((N_Z - 1, 2 * hd, 128), BF16),
        pltpu.VMEM((N_OUTER, 32, 2 * hd), F32),
        pltpu.VMEM((2, 32, 2 * hd), F32),
        dma((3,)), dma((3,)), dma((3,)), dma((3,)),
        dma((N_Z,)), dma((N_Z,)), dma((N_Z,)), dma, dma, dma, dma((2,)), dma((2,)),
        dma((N_Z,)), dma((N_Z,)), dma((N_Z,)), dma((2, N_Z)),
        dma((N_Z - 1,)), dma((N_Z - 1,)), dma((3,)), dma((2,)),
    ]
    query_out, input_grad, weight_grad = pl.pallas_call(
        kernel,
        out_shape=[
            jax.ShapeDtypeStruct((rows, hd), BF16),
            jax.ShapeDtypeStruct((tok, width // 2), BF16),
            jax.ShapeDtypeStruct((64, hd), F32),
        ],
        in_specs=[vmem, vmem, vmem, smem, hbm, hbm],
        out_specs=[vmem, vmem, vmem],
        scratch_shapes=scratch,
        compiler_params=pltpu.CompilerParams(
            collective_id=0, has_side_effects=True, vmem_limit_bytes=60 * 2**20
        ),
        name="backward",
    )(
        queries.reshape(rows, hd),
        grad_out.reshape(rows, hd),
        keys_values.reshape(tok * 2, hd),
        block_order,
        inputs,
        kv_weight.reshape(width * 2, hd),
    )
    return (
        query_out.reshape(queries.shape),
        input_grad,
        weight_grad.reshape(32, 1, 2, hd),
    )


def solution(mesh):
    return jax.shard_map(
        shards,
        mesh=mesh,
        in_specs=(
            P(None, ("inner", "outer"), "head", None, None),
            P(None, ("inner", "outer"), "head", None, None),
            P(("inner", "outer"), "head", None, None),
            P(("inner", "outer"), None),
            P(None, "head", None, None),
            P(),
        ),
        out_specs=(
            P(None, ("inner", "outer"), "head", None, None),
            P(("inner", "outer"), "head"),
            P(("inner", "outer"), "head", None, None),
        ),
        check_vma=False,
    )
```

time: 1420 us -> 73.9 us (0.05)
  waiting for transfers between devices: 1300 us -> 0 us
  Pallas kernels: 0 us -> 68.9 us
  matrix products: 49 us -> 0 us
  between operations: 20 us -> 0.66 us
  starting transfers between devices: 17.6 us -> 0 us
  other arithmetic: 16.7 us -> 0 us
    unnamed x3 -> x0, waiting for transfers between devices: 1290 us -> none
    pallas_call x0 -> x1, Pallas kernels: none -> 68.9 us  [shards(): pl.pallas_call(kernel, out_shape=[jax.ShapeDtypeStruct((rows, hd), BF16),...]
    dot_general x42 -> x0, matrix products: 49 us -> none  [the longest x8 16.1 us: block_scores(): jnp.einsum('lthd,sd->lhts', grad_rows, values_only, preferred_element_typ...]
    ppermute x9 -> x0, starting transfers between devices: 17.2 us -> none  [passed_along(): lax.ppermute(array, axis, [(i, (i + by) % count) for i in range(count)])]
  transfers between devices with their start and end apart: 11 -> 0, of which waited for: 4 -> 0; matrix products, arithmetic and copies ran while one was open for 2% -> 0% of each run, Pallas kernels for 0% -> 0%
where the time goes in v1:
time: 73.9 us; the launch traced here: 73.8 us
  Pallas kernels  68.9 us (93%)
  local copies, waits for them, and re-layouts  4.17 us (6%)
    pallas_call x1, Pallas kernels, shards(): pl.pallas_call(kernel, out_shape=[jax.ShapeDtypeStruct((rows, hd), BF16),...  68.9 us
    unnamed x7, local copies, waits for them, and re-layouts  4.17 us

profile of v1, /device:TPU:1, one launch (start us, length us, event | category | flops | bytes accessed | tf_op | source)
XLA Modules:
  0.0 73.8 jit_solution(8485635194022813271)
XLA Ops:
  0.6 68.9 %backward.1 = (bf16[3072,128]{1,0:T(8,128)(2,1)}, bf16[384,2048]{1,0:T(8,128)(2,1)}, f32[64,128]{1,0:T(8,128)}) custom-call(bf16[3072,128]{1,0:T(8,128)(2,1)} %bitcast.12, bf16[3072,128]{1,0:T(8,128)(2,1)} %bitcast.13, bf16[768,128]{1,0:T(8,128)(2,1)} %bitcast.14, s32[128]{0:T(128)} %order.1, bf16[384,4096]{1,0:T(8,128)(2,1)} %inputs.1, ...), custom_call_target="tpu_custom_call" | custom-call | tf_op jit(solution)/shard_map/backward/pallas_call | solution.py:434
  69.6 0.0 copy-start
  69.6 0.0 copy-start.1
  69.6 2.4 %copy.14 = bf16[2,384,1,4,128]{4,3,2,1,0:T(4,128)(2,1)} copy(bf16[2,384,1,4,128]{4,3,2,1,0:T(4,128)(2,1)} %bitcast.11) | data formatting | bytes 1572864
  72.0 0.0 copy-done
  72.0 1.1 %copy.15 = bf16[384,2048]{1,0:T(8,128)(2,1)} copy(bf16[384,2048]{1,0:T(8,128)(2,1)S(1)} %copy-done) | data formatting | bytes 3145728
  73.1 0.0 copy-done.1
  73.1 0.6 copy.16
Async XLA Ops:
  69.6 2.4 %copy-start = (bf16[384,2048]{1,0:T(8,128)(2,1)S(1)}, bf16[384,2048]{1,0:T(8,128)(2,1)}, u32[]{:S(2)}) copy-start(bf16[384,2048]{1,0:T(8,128)(2,1)} %get-tuple-element.16) | copy-start | bytes 4718596
  69.6 3.6 %copy-start.1 = (f32[64,128]{1,0:T(8,128)S(1)}, f32[64,128]{1,0:T(8,128)}, u32[]{:S(2)}) copy-start(f32[64,128]{1,0:T(8,128)} %get-tuple-element.8) | copy-start | bytes 98308

commit v2 on v1

v2 whole, which is shorter than its diff:
```python
import functools
import math

import jax
import jax.numpy as jnp
from jax import lax
from jax.experimental import pallas as pl
from jax.experimental.pallas import tpu as pltpu
from jax.sharding import PartitionSpec as P

F32 = jnp.float32
BF16 = jnp.bfloat16
MESH = pl.DeviceIdType.MESH
N_INNER = 32
N_Y = 4
N_Z = 8
N_OUTER = 4
NT = (((1,), (1,)), ((), ()))
NN = (((1,), (0,)), ((), ()))
FAR = -1e30
TILE = 512


def dot(a, b, dims):
    return lax.dot_general(a, b, dims, preferred_element_type=F32)


def remote(src, dst, send, recv, **where):
    return pltpu.make_async_remote_copy(
        src_ref=src,
        dst_ref=dst,
        send_sem=send,
        recv_sem=recv,
        device_id=where,
        device_id_type=MESH,
    )


def kernel(
    q, go, kv_raw, order, inputs, weight,
    dq, ig, wg,
    E, DP, top, total, delta, fac, k_t, kv, kv_mid, gout, gin, inp, w_own, w_oth, w_cat,
    pair, pair_t, ysend, yrecv, yacc, zsend, zrecv, fsend, frecv,
    kv_ss, kv_rs, g_ss, g_rs, in_ls, in_ss, in_rs, w_ls, w_ss, w_rs, p_ss, p_rs,
    y_ss, y_rs, z_ss, z_rs, f_ss, f_rs,
):
    rows = q.shape[0]
    tok = kv.shape[2]
    hd = kv.shape[3]
    group = rows // 2 // tok
    scale = 1.0 / math.sqrt(hd)
    scale2 = scale * math.log2(math.e)
    half_w = w_own.shape[0]
    half_d = half_w // 2
    steps = rows // TILE
    cut = TILE // group
    i = lax.axis_index("inner")
    o = lax.axis_index("outer")
    h = lax.axis_index("head")
    z = i // N_Y
    y = lax.rem(i, N_Y)
    c = lax.rem(o, 2)

    def inner(by):
        return lax.rem(i + by + N_INNER, N_INNER)

    def outer(by):
        return lax.rem(o + by + N_OUTER, N_OUTER)

    def at_z(by):
        return lax.rem(z + by, N_Z) * N_Y + y

    def at_y(place):
        return z * N_Y + place

    core_mate = o + 1 - 2 * c
    relay_to = lax.rem(at_y(lax.rem(y + 1, N_Y)) + 2, N_INNER)
    two_back = inner(-2)
    relay_from = two_back // N_Y * N_Y + lax.rem(lax.rem(two_back, N_Y) + 3, N_Y)

    barrier = pltpu.get_barrier_semaphore()
    greeted = [{"inner": inner(by)} for by in (1, 2, -1, -2)]
    greeted += [{"outer": outer(by)} for by in (1, 2, 3)]
    greeted += [{"head": 1 - h}, {"inner": relay_to}, {"inner": relay_from}]
    greeted += [{"inner": at_y(lax.rem(y + by, N_Y))} for by in (1, 2, 3)]
    greeted += [{"inner": at_z(by)} for by in range(1, N_Z)]
    for where in greeted:
        pl.semaphore_signal(barrier, inc=1, device_id=where, device_id_type=MESH)

    kv[0, 0] = kv_raw[pl.ds(0, tok, 2), :]
    kv[0, 1] = kv_raw[pl.ds(1, tok, 2), :]
    w_local = pltpu.make_async_copy(
        weight.at[pl.ds(pl.multiple_of(h * half_w, half_w), half_w), :], w_own, w_ls
    )
    w_local.start()

    def in_local(zz):
        return pltpu.make_async_copy(
            inputs.at[:, pl.ds(pl.multiple_of(zz * 512 + c * 256, 256), 256)],
            inp.at[zz, pl.ds(0, tok), :],
            in_ls.at[zz],
        )

    def in_remote(zz):
        return remote(
            inputs.at[:, pl.ds(pl.multiple_of(zz * 512 + (1 - c) * 256, 256), 256)],
            inp.at[zz, pl.ds(tok, tok), :],
            in_ss.at[zz],
            in_rs.at[zz],
            outer=core_mate,
        )

    for zz in range(N_Z):
        in_local(zz).start()
    pl.semaphore_wait(barrier, len(greeted))

    one = remote(kv.at[0], kv.at[1], kv_ss.at[0], kv_rs.at[0], inner=inner(1))
    keys_two = remote(kv.at[0, 0], kv.at[2, 0], kv_ss.at[1], kv_rs.at[1], inner=inner(2))
    values_mid = remote(
        kv.at[0, 1], kv_mid, kv_ss.at[2], kv_rs.at[2], inner=at_y(lax.rem(y + 3, N_Y))
    )
    values_two = remote(kv_mid, kv.at[2, 1], kv_ss.at[3], kv_rs.at[3], inner=relay_to)
    sideways = remote(kv.at[0], kv.at[3], kv_ss.at[4], kv_rs.at[4], outer=outer(1))
    forward = [values_mid, one, sideways, keys_two, values_two]
    for copy in forward[:4]:
        copy.start()

    def back(part, b):
        to = ({"inner": inner(-1)}, {"inner": inner(-2)}, {"outer": outer(-1)})[b - 1]
        at = (part, b - 1)
        return remote(gout.at[at], gin.at[at], g_ss.at[at], g_rs.at[at], **to)

    quarter = pl.ds(pl.multiple_of(c * (half_w // 2), half_w // 2), half_w // 2)
    w_remote = remote(
        weight.at[pl.ds(pl.multiple_of((1 - h) * half_w + c * (half_w // 2), half_w // 2), half_w // 2), :],
        w_oth.at[quarter, :],
        w_ss.at[0],
        w_rs.at[0],
        head=1 - h,
    )
    w_mate = remote(
        w_oth.at[quarter, :], w_oth.at[quarter, :], w_ss.at[1], w_rs.at[1], outer=core_mate
    )
    for zz in range(N_Z):
        in_remote(zz).start()

    mine = order[i * N_OUTER + o]
    block_ids = [None, inner(-1) * N_OUTER + o, inner(-2) * N_OUTER + o, i * N_OUTER + outer(-1)]
    bias = [None]
    for block_id in block_ids[1:]:
        bias.append(jnp.where(order[block_id] < mine, 0.0, FAR).astype(F32))

    def tile(t):
        return pl.ds(pl.multiple_of(t * TILE, TILE), TILE)

    def look_own():
        key = lax.broadcasted_iota(jnp.int32, (cut, TILE), 0)
        row = lax.broadcasted_iota(jnp.int32, (cut, TILE), 1)
        seen = key <= row // group
        for t in range(steps):
            cs = pl.ds(t * TILE, TILE)
            n = (t * cut) % tok + cut
            s = dot(kv[0, 0, :n, :], q[cs, :], NT)
            last = jnp.where(seen, s[n - cut :], FAR)
            s = last if n == cut else jnp.concatenate([s[: n - cut], last], axis=0)
            dp = dot(kv[0, 1, :n, :], go[cs, :], NT)
            here = jnp.max(s, axis=0, keepdims=True) * scale2
            e = jnp.exp2(s * scale2 - here)
            E[0, :n, cs] = e
            DP[0, :n, cs] = dp
            if n < tok:
                E[0, n:, cs] = jnp.zeros((tok - n, TILE), F32)
            top[0, :, cs] = here
            total[:, cs] = jnp.sum(e, axis=0, keepdims=True)
            delta[:, cs] = jnp.sum(e * dp, axis=0, keepdims=True)

    def look(b, before):
        def body(t, carry):
            cs = tile(t)
            s = dot(kv[b, 0], q[cs, :], NT)
            dp = dot(kv[b, 1], go[cs, :], NT)
            old = top[before, :, cs]
            new = jnp.maximum(old, jnp.max(s, axis=0, keepdims=True) * scale2 + bias[b])
            factor = jnp.exp2(old - new)
            e = jnp.exp2(s * scale2 - (new - bias[b]))
            E[b, :, cs] = e
            DP[b, :, cs] = dp
            top[b, :, cs] = new
            total[:, cs] = total[:, cs] * factor + jnp.sum(e, axis=0, keepdims=True)
            delta[:, cs] = delta[:, cs] * factor + jnp.sum(e * dp, axis=0, keepdims=True)
            return carry

        lax.fori_loop(0, steps, body, 0, unroll=2)

    def value_step(b, n, cs):
        p = (E[b, :n, cs] * fac[b, :, cs]).astype(BF16)
        return dot(p, go[cs, :], NN)

    def key_step(b, n, cs):
        ds = E[b, :n, cs] * fac[b, :, cs] * (DP[b, :n, cs] - delta[:, cs])
        E[b, :n, cs] = ds
        return dot(ds.astype(BF16), q[cs, :], NN)

    def block_sum(step, b):
        if b > 0:
            def body(t, total_so_far):
                return total_so_far + step(b, tok, tile(t))

            return lax.fori_loop(0, steps, body, jnp.zeros((tok, hd), F32), unroll=2)
        parts = [None] * (tok // cut)
        for t in range(steps):
            n = (t * cut) % tok + cut
            x = step(0, n, pl.ds(t * TILE, TILE))
            for k in range(n // cut):
                piece = x[k * cut : k * cut + cut]
                parts[k] = piece if parts[k] is None else parts[k] + piece
        return jnp.concatenate(parts, axis=0)

    look_own()
    values_mid.wait_recv()
    values_two.start()
    sideways.wait_recv()
    w_remote.start()
    look(3, 0)
    one.wait_recv()
    look(1, 3)
    keys_two.wait_recv()
    values_two.wait_recv()
    look(2, 1)
    sums = total[...]
    delta[...] = delta[...] / sums
    lse = top[2] + jnp.log2(sums)
    for b in range(4):
        fac[b] = jnp.exp2(top[b] - lse)

    def to_core(part):
        at = (part, 0)
        return remote(pair.at[at], pair.at[part, 1], p_ss.at[at], p_rs.at[at], outer=core_mate)

    def to_head(part):
        at = (part, 1)
        return remote(pair.at[part, 0], pair.at[part, 2], p_ss.at[at], p_rs.at[at], head=1 - h)

    def send_back(part, b, grad):
        gout[part, b - 1] = grad.astype(BF16)
        back(part, b).start()

    def finish_pair(part, grad):
        for b in (2, 1, 3):
            back(part, b).wait_recv()
            grad = grad + gin[part, b - 1].astype(F32)
        pair[part, 0] = grad.astype(BF16)
        to_core(part).start()
        to_head(part).start()
        pair_t[part, :, :tok] = grad.T.astype(BF16)

    owner = y // 2 == c
    not_owner = y // 2 != c

    def z_at(zz):
        return lax.rem(z + 1 + zz, N_Z)

    def above(j):
        return lax.rem(y - (2 * c + j) + N_Y, N_Y)

    def y_copy(part, j, zz):
        return remote(
            ysend.at[part, j, zz],
            yrecv.at[part, above(j) - 1, zz],
            y_ss.at[part, j, zz],
            y_rs.at[part, above(j) - 1, zz],
            inner=at_y(2 * c + j),
        )

    def y_arrival(part, k, zz):
        return remote(
            ysend.at[part, 0, zz], yrecv.at[part, k, zz], y_ss.at[part, 0, zz],
            y_rs.at[part, k, zz], inner=at_y(lax.rem(y + 1, N_Y)),
        )

    def z_copy(part, zz):
        at = (part, zz)
        return remote(
            zsend.at[at], zrecv.at[at], z_ss.at[at], z_rs.at[at], inner=z_at(zz) * N_Y + y
        )

    def produce(part):
        to_core(part).wait_recv()
        pair_t[part, :, tok:] = pair[part, 1].astype(F32).T.astype(BF16)

        def body(zz, carry):
            x = dot(pair_t[part], inp[z_at(zz)], NN)
            for j in range(2):
                piece = x[:, j * hd : j * hd + hd]

                @pl.when(above(j) == 0)
                def _(piece=piece):
                    yacc[part, zz] = piece

                @pl.when(above(j) != 0)
                def _(piece=piece, j=j):
                    ysend[part, j, zz] = piece.astype(BF16)
                    y_copy(part, j, zz).start()

            return carry

        lax.fori_loop(0, N_Z, body, 0, unroll=2)

    def gather_y(part):
        @pl.when(owner)
        def _():
            def body(zz, carry):
                x = yacc[part, zz]
                for k in range(3):
                    y_arrival(part, k, zz).wait_recv()
                    x = x + yrecv[part, k, zz].astype(F32)
                yacc[part, zz] = x

                @pl.when(zz < N_Z - 1)
                def _():
                    zsend[part, zz] = x.astype(BF16)
                    z_copy(part, zz).start()

                return carry

            lax.fori_loop(0, N_Z, body, 0)

    def gather_z(part):
        @pl.when(owner)
        def _():
            def body(zz, x):
                z_copy(part, zz).wait_recv()
                return x + zrecv[part, zz].astype(F32)

            x = lax.fori_loop(0, N_Z - 1, body, yacc[part, N_Z - 1])
            x = x.T / math.sqrt(tok * N_INNER * N_OUTER)
            for place in range(N_OUTER):
                fsend[place, :, part * hd : part * hd + hd] = x[place * 32 : place * 32 + 32, :]

    for b in (2, 1, 3):
        send_back(1, b, block_sum(value_step, b))
    values_own = block_sum(value_step, 0)
    send_back(0, 2, block_sum(key_step, 2) * scale)
    finish_pair(1, values_own)
    w_remote.wait_recv()
    w_mate.start()
    send_back(0, 1, block_sum(key_step, 1) * scale)
    for zz in range(N_Z):
        in_local(zz).wait()
        in_remote(zz).wait_recv()
    produce(1)
    send_back(0, 3, block_sum(key_step, 3) * scale)
    finish_pair(0, block_sum(key_step, 0) * scale)
    gather_y(1)
    produce(0)

    for b in range(4):
        k_t[:, b * tok : b * tok + tok] = kv[b, 0].astype(F32).T.astype(BF16)

    def finish_queries(t, carry):
        cs = tile(t)
        ds = E[:, :, cs].reshape(4 * tok, TILE).astype(BF16)
        dq[cs, :] = (dot(k_t[...], ds, NN) * scale).T.astype(BF16)
        return carry

    lax.fori_loop(0, steps, finish_queries, 0, unroll=2)
    gather_y(0)
    w_local.wait()
    w_mate.wait_recv()
    for k, w in enumerate((w_own, w_oth)):
        w_cat[k, :, :hd] = w[pl.ds(0, half_d, 2), :]
        w_cat[k, :, hd:] = w[pl.ds(1, half_d, 2), :]
    to_head(1).wait_recv()
    to_head(0).wait_recv()

    def input_part(t, carry):
        cs = tile(t)
        term = jnp.zeros((tok, TILE), F32)
        for k, at in enumerate((0, 2)):
            both = jnp.concatenate([pair[0, at], pair[1, at]], axis=1)
            term = term + dot(both, w_cat[k, cs, :], NT)
        ig[:, cs] = term.astype(BF16)
        return carry

    lax.fori_loop(0, half_d // TILE, input_part, 0, unroll=2)
    gather_z(1)
    gather_z(0)

    def fin_copy(by):
        place = (core_mate, lax.rem(o + 2, N_OUTER), N_OUTER - 1 - o)[by - 1]
        slot = 0 if by == 1 else 1
        return remote(
            fsend.at[place], frecv.at[slot], f_ss.at[by - 1], f_rs.at[slot], outer=place
        )

    @pl.when(owner)
    def _():
        for by in (3, 2, 1):
            fin_copy(by).start()
        fin_copy(2).wait_recv()
        x = fsend[o] + frecv[1]
        wg[pl.ds(0, 32, 2), :] = x[:, :hd]
        wg[pl.ds(1, 32, 2), :] = x[:, hd:]

    @pl.when(not_owner)
    def _():
        fin_copy(1).wait_recv()
        fin_copy(3).wait_recv()
        x = frecv[0] + frecv[1]
        wg[pl.ds(0, 32, 2), :] = x[:, :hd]
        wg[pl.ds(1, 32, 2), :] = x[:, hd:]

    for copy in forward + [w_remote, w_mate]:
        copy.wait_send()
    for part in range(2):
        to_core(part).wait_send()
        to_head(part).wait_send()
        for b in (1, 2, 3):
            back(part, b).wait_send()

    def sent(zz, carry):
        in_remote(zz).wait_send()
        for part in range(2):
            for j in range(2):

                @pl.when(above(j) != 0)
                def _(part=part, j=j):
                    y_copy(part, j, zz).wait_send()

        return carry

    lax.fori_loop(0, N_Z, sent, 0)

    @pl.when(owner)
    def _():
        for zz in range(N_Z - 1):
            for part in range(2):
                z_copy(part, zz).wait_send()
        for by in (1, 2, 3):
            fin_copy(by).wait_send()


def shards(queries, grad_out, keys_values, inputs, kv_weight, block_order):
    layers, tok, _, per_group, hd = queries.shape
    rows = layers * tok * per_group
    width = inputs.shape[1]
    vmem = pl.BlockSpec(memory_space=pltpu.VMEM)
    smem = pl.BlockSpec(memory_space=pltpu.SMEM)
    hbm = pl.BlockSpec(memory_space=pl.ANY)
    dma = pltpu.SemaphoreType.DMA
    scratch = [
        pltpu.VMEM((4, tok, rows), F32),
        pltpu.VMEM((4, tok, rows), F32),
        pltpu.VMEM((4, 1, rows), F32),
        pltpu.VMEM((1, rows), F32),
        pltpu.VMEM((1, rows), F32),
        pltpu.VMEM((4, 1, rows), F32),
        pltpu.VMEM((hd, 4 * tok), BF16),
        pltpu.VMEM((4, 2, tok, hd), BF16),
        pltpu.VMEM((tok, hd), BF16),
        pltpu.VMEM((2, 3, tok, hd), BF16),
        pltpu.VMEM((2, 3, tok, hd), BF16),
        pltpu.VMEM((N_Z, 2 * tok, 256), BF16),
        pltpu.VMEM((width, hd), BF16),
        pltpu.VMEM((width, hd), BF16),
        pltpu.VMEM((2, width // 2, 2 * hd), BF16),
        pltpu.VMEM((2, 3, tok, hd), BF16),
        pltpu.VMEM((2, hd, 2 * tok), BF16),
        pltpu.VMEM((2, 2, N_Z, hd, 128), BF16),
        pltpu.VMEM((2, 3, N_Z, hd, 128), BF16),
        pltpu.VMEM((2, N_Z, hd, 128), F32),
        pltpu.VMEM((2, N_Z - 1, hd, 128), BF16),
        pltpu.VMEM((2, N_Z - 1, hd, 128), BF16),
        pltpu.VMEM((N_OUTER, 32, 2 * hd), F32),
        pltpu.VMEM((2, 32, 2 * hd), F32),
        dma((5,)), dma((5,)), dma((2, 3)), dma((2, 3)),
        dma((N_Z,)), dma((N_Z,)), dma((N_Z,)), dma, dma((2,)), dma((2,)), dma((2, 2)), dma((2, 2)),
        dma((2, 2, N_Z)), dma((2, 3, N_Z)),
        dma((2, N_Z - 1)), dma((2, N_Z - 1)), dma((3,)), dma((2,)),
    ]
    query_out, input_grad, weight_grad = pl.pallas_call(
        kernel,
        out_shape=[
            jax.ShapeDtypeStruct((rows, hd), BF16),
            jax.ShapeDtypeStruct((tok, width // 2), BF16),
            jax.ShapeDtypeStruct((64, hd), F32),
        ],
        in_specs=[vmem, vmem, vmem, smem, hbm, hbm],
        out_specs=[vmem, vmem, vmem],
        scratch_shapes=scratch,
        compiler_params=pltpu.CompilerParams(
            collective_id=0, has_side_effects=True, vmem_limit_bytes=60 * 2**20
        ),
        name="backward",
    )(
        queries.reshape(rows, hd),
        grad_out.reshape(rows, hd),
        keys_values.reshape(tok * 2, hd),
        block_order,
        inputs,
        kv_weight.reshape(width * 2, hd),
    )

    def handover(x, y, a, x_out, y_out, a_out, xs, ys, as_, r_sem, w_sem):
        parts = []
        for src, mid, dst, cuts in ((x, xs, x_out, 4), (y, ys, y_out, 4), (a, as_, a_out, 1)):
            n = src.shape[0] // cuts
            for k in range(cuts):
                at = pl.ds(k * n, n)
                parts.append((src.at[at, :], mid.at[at, :], dst.at[at, :]))
        reads = [pltpu.make_async_copy(s, m, r_sem.at[k]) for k, (s, m, _) in enumerate(parts)]
        writes = [pltpu.make_async_copy(m, d, w_sem.at[k]) for k, (_, m, d) in enumerate(parts)]
        for copy in reads:
            copy.start()
        for k, copy in enumerate(writes):
            reads[k].wait()
            copy.start()
        for copy in writes:
            copy.wait()

    query_out, input_grad, weight_grad = pl.pallas_call(
        handover,
        out_shape=[
            jax.ShapeDtypeStruct(query_out.shape, BF16),
            jax.ShapeDtypeStruct(input_grad.shape, BF16),
            jax.ShapeDtypeStruct((64, hd), F32),
        ],
        in_specs=[hbm, hbm, hbm],
        out_specs=[hbm, hbm, hbm],
        scratch_shapes=[
            pltpu.VMEM(query_out.shape, BF16),
            pltpu.VMEM(input_grad.shape, BF16),
            pltpu.VMEM((64, hd), F32),
            dma((9,)),
            dma((9,)),
        ],
        compiler_params=pltpu.CompilerParams(vmem_limit_bytes=60 * 2**20),
        name="handover",
    )(query_out, input_grad, weight_grad)

    return (
        query_out.reshape(queries.shape),
        input_grad,
        weight_grad.reshape(32, 1, 2, hd),
    )


def solution(mesh):
    return jax.shard_map(
        shards,
        mesh=mesh,
        in_specs=(
            P(None, ("inner", "outer"), "head", None, None),
            P(None, ("inner", "outer"), "head", None, None),
            P(("inner", "outer"), "head", None, None),
            P(("inner", "outer"), None),
            P(None, "head", None, None),
            P(),
        ),
        out_specs=(
            P(None, ("inner", "outer"), "head", None, None),
            P(("inner", "outer"), "head"),
            P(("inner", "outer"), "head", None, None),
        ),
        check_vma=False,
    )
```

time: 73.9 us -> 66.5 us (0.90)
  local copies, waits for them, and re-layouts: 4.17 us -> 0 us
  Pallas kernels: 68.9 us -> 65.7 us
    pallas_call x1, Pallas kernels: 68.9 us -> 63 us  [shards(): pl.pallas_call(kernel, out_shape=[jax.ShapeDtypeStruct((rows, hd), BF16),...]
    unnamed x7 -> x0, local copies, waits for them, and re-layouts: 4.17 us -> none
    pallas_call x0 -> x1, Pallas kernels: none -> 2.64 us  [shards(): pl.pallas_call(handover, out_shape=[jax.ShapeDtypeStruct(query_out.shape,...]
where the time goes in v2:
time: 66.5 us; the launch traced here: 66.3 us
  Pallas kernels  65.7 us (99%)
    pallas_call x1, Pallas kernels, shards(): pl.pallas_call(kernel, out_shape=[jax.ShapeDtypeStruct((rows, hd), BF16),...  63 us
    pallas_call x1, Pallas kernels, shards(): pl.pallas_call(handover, out_shape=[jax.ShapeDtypeStruct(query_out.shape,...  2.64 us

profile of v2, /device:TPU:1, one launch (start us, length us, event | category | flops | bytes accessed | tf_op | source)
XLA Modules:
  0.0 66.3 jit_solution(4219773842648449534)
XLA Ops:
  0.6 63.0 %backward.1 = (bf16[3072,128]{1,0:T(8,128)(2,1)}, bf16[384,2048]{1,0:T(8,128)(2,1)}, f32[64,128]{1,0:T(8,128)}) custom-call(bf16[3072,128]{1,0:T(8,128)(2,1)} %bitcast.11, bf16[3072,128]{1,0:T(8,128)(2,1)} %bitcast.12, bf16[768,128]{1,0:T(8,128)(2,1)} %bitcast.13, s32[128]{0:T(128)} %order.1, bf16[384,4096]{1,0:T(8,128)(2,1)} %inputs.1, ...), custom_call_target="tpu_custom_call" | custom-call | tf_op jit(solution)/shard_map/backward/pallas_call | solution.py:481
  63.7 2.6 %handover.1 = (bf16[3072,128]{1,0:T(8,128)(2,1)}, bf16[384,2048]{1,0:T(8,128)(2,1)}, f32[64,128]{1,0:T(8,128)}) custom-call(bf16[3072,128]{1,0:T(8,128)(2,1)} %get-tuple-element.9.x, bf16[384,2048]{1,0:T(8,128)(2,1)} %get-tuple-element.10.y, f32[64,128]{1,0:T(8,128)} %get-tuple-element.11.a), custom_call_target="tpu_custom_call" | custom-call | tf_op jit(solution)/shard_map/handover/pallas_call | solution.py:521

commit v3 on v2

--- a/solution.py
+++ b/solution.py
@@ -37,12 +37,13 @@
 
 
 def kernel(
-    q, go, kv_raw, order, inputs, weight,
-    dq, ig, wg,
+    q_hbm, go_hbm, kv_raw, order, inputs, weight,
+    dq_hbm, ig_hbm, wg,
+    q, go, dq, ig,
     E, DP, top, total, delta, fac, k_t, kv, kv_mid, gout, gin, inp, w_own, w_oth, w_cat,
-    pair, pair_t, ysend, yrecv, yacc, zsend, zrecv, fsend, frecv,
+    pair, pair_t, ysend, yrecv, yacc, zsend, zrecv, zacc,
     kv_ss, kv_rs, g_ss, g_rs, in_ls, in_ss, in_rs, w_ls, w_ss, w_rs, p_ss, p_rs,
-    y_ss, y_rs, z_ss, z_rs, f_ss, f_rs,
+    y_ss, y_rs, z_ss, z_rs, ready, io_s,
 ):
     rows = q.shape[0]
     tok = kv.shape[2]
@@ -87,12 +88,17 @@
     for where in greeted:
         pl.semaphore_signal(barrier, inc=1, device_id=where, device_id_type=MESH)
 
+    q_in = pltpu.make_async_copy(q_hbm, q, io_s.at[0])
+    go_in = pltpu.make_async_copy(go_hbm, go, io_s.at[1])
+    dq_out = pltpu.make_async_copy(dq, dq_hbm, io_s.at[2])
+    ig_out = pltpu.make_async_copy(ig, ig_hbm, io_s.at[3])
+    q_in.start()
+    go_in.start()
     kv[0, 0] = kv_raw[pl.ds(0, tok, 2), :]
     kv[0, 1] = kv_raw[pl.ds(1, tok, 2), :]
     w_local = pltpu.make_async_copy(
         weight.at[pl.ds(pl.multiple_of(h * half_w, half_w), half_w), :], w_own, w_ls
     )
-    w_local.start()
 
     def in_local(zz):
         return pltpu.make_async_copy(
@@ -110,8 +116,6 @@
             outer=core_mate,
         )
 
-    for zz in range(N_Z):
-        in_local(zz).start()
     pl.semaphore_wait(barrier, len(greeted))
 
     one = remote(kv.at[0], kv.at[1], kv_ss.at[0], kv_rs.at[0], inner=inner(1))
@@ -141,7 +145,11 @@
     w_mate = remote(
         w_oth.at[quarter, :], w_oth.at[quarter, :], w_ss.at[1], w_rs.at[1], outer=core_mate
     )
+    for by in range(1, N_Z):
+        pl.semaphore_signal(ready, inc=1, device_id={"inner": at_z(by)}, device_id_type=MESH)
+    w_local.start()
     for zz in range(N_Z):
+        in_local(zz).start()
         in_remote(zz).start()
 
     mine = order[i * N_OUTER + o]
@@ -216,6 +224,8 @@
                 parts[k] = piece if parts[k] is None else parts[k] + piece
         return jnp.concatenate(parts, axis=0)
 
+    q_in.wait()
+    go_in.wait()
     look_own()
     values_mid.wait_recv()
     values_two.start()
@@ -278,10 +288,21 @@
             y_rs.at[part, k, zz], inner=at_y(lax.rem(y + 1, N_Y)),
         )
 
-    def z_copy(part, zz):
-        at = (part, zz)
+    def z_copy(part, zz, place):
+        slot = 2 * zz + jnp.where(o // 2 == place // 2, 0, 1)
         return remote(
-            zsend.at[at], zrecv.at[at], z_ss.at[at], z_rs.at[at], inner=z_at(zz) * N_Y + y
+            zsend.at[part, zz, pl.ds(place * 32, 32), :],
+            zrecv.at[part, slot],
+            z_ss.at[part, zz, place],
+            z_rs.at[part, slot],
+            inner=z_at(zz) * N_Y + y,
+            outer=place,
+        )
+
+    def z_arrival(part, slot):
+        return remote(
+            zsend.at[part, 0, pl.ds(0, 32), :], zrecv.at[part, slot], z_ss.at[part, 0, 0],
+            z_rs.at[part, slot], inner=z_at(0) * N_Y + y,
         )
 
     def produce(part):
@@ -314,28 +335,39 @@
                 for k in range(3):
                     y_arrival(part, k, zz).wait_recv()
                     x = x + yrecv[part, k, zz].astype(F32)
-                yacc[part, zz] = x
-
-                @pl.when(zz < N_Z - 1)
+                x = x.T
+                zsend[part, zz] = x.astype(BF16)
+                for place in range(N_OUTER):
+
+                    @pl.when((zz < N_Z - 1) | (place != o))
+                    def _(place=place):
+                        z_copy(part, zz, place).start()
+
+                @pl.when(zz == N_Z - 1)
                 def _():
-                    zsend[part, zz] = x.astype(BF16)
-                    z_copy(part, zz).start()
+                    for place in range(N_OUTER):
+
+                        @pl.when(place == o)
+                        def _(place=place):
+                            zacc[part] = x[place * 32 : place * 32 + 32, :]
 
                 return carry
 
             lax.fori_loop(0, N_Z, body, 0)
 
     def gather_z(part):
-        @pl.when(owner)
+        @pl.when(not_owner)
         def _():
-            def body(zz, x):
-                z_copy(part, zz).wait_recv()
-                return x + zrecv[part, zz].astype(F32)
-
-            x = lax.fori_loop(0, N_Z - 1, body, yacc[part, N_Z - 1])
-            x = x.T / math.sqrt(tok * N_INNER * N_OUTER)
-            for place in range(N_OUTER):
-                fsend[place, :, part * hd : part * hd + hd] = x[place * 32 : place * 32 + 32, :]
+            z_arrival(part, 2 * N_Z - 2).wait_recv()
+            zacc[part] = zrecv[part, 2 * N_Z - 2].astype(F32)
+
+        def body(slot, x):
+            z_arrival(part, slot).wait_recv()
+            return x + zrecv[part, slot].astype(F32)
+
+        x = lax.fori_loop(0, 2 * N_Z - 2, body, zacc[part])
+        x = body(2 * N_Z - 1, x) / math.sqrt(tok * N_INNER * N_OUTER)
+        wg[pl.ds(part, 32, 2), :] = x
 
     for b in (2, 1, 3):
         send_back(1, b, block_sum(value_step, b))
@@ -351,6 +383,7 @@
     produce(1)
     send_back(0, 3, block_sum(key_step, 3) * scale)
     finish_pair(0, block_sum(key_step, 0) * scale)
+    pl.semaphore_wait(ready, N_Z - 1)
     gather_y(1)
     produce(0)
 
@@ -364,6 +397,7 @@
         return carry
 
     lax.fori_loop(0, steps, finish_queries, 0, unroll=2)
+    dq_out.start()
     gather_y(0)
     w_local.wait()
     w_mate.wait_recv()
@@ -383,32 +417,9 @@
         return carry
 
     lax.fori_loop(0, half_d // TILE, input_part, 0, unroll=2)
+    ig_out.start()
     gather_z(1)
     gather_z(0)
-
-    def fin_copy(by):
-        place = (core_mate, lax.rem(o + 2, N_OUTER), N_OUTER - 1 - o)[by - 1]
-        slot = 0 if by == 1 else 1
-        return remote(
-            fsend.at[place], frecv.at[slot], f_ss.at[by - 1], f_rs.at[slot], outer=place
-        )
-
-    @pl.when(owner)
-    def _():
-        for by in (3, 2, 1):
-            fin_copy(by).start()
-        fin_copy(2).wait_recv()
-        x = fsend[o] + frecv[1]
-        wg[pl.ds(0, 32, 2), :] = x[:, :hd]
-        wg[pl.ds(1, 32, 2), :] = x[:, hd:]
-
-    @pl.when(not_owner)
-    def _():
-        fin_copy(1).wait_recv()
-        fin_copy(3).wait_recv()
-        x = frecv[0] + frecv[1]
-        wg[pl.ds(0, 32, 2), :] = x[:, :hd]
-        wg[pl.ds(1, 32, 2), :] = x[:, hd:]
 
     for copy in forward + [w_remote, w_mate]:
         copy.wait_send()
@@ -433,11 +444,20 @@
 
     @pl.when(owner)
     def _():
-        for zz in range(N_Z - 1):
+        def sent_z(zz, carry):
             for part in range(2):
-                z_copy(part, zz).wait_send()
-        for by in (1, 2, 3):
-            fin_copy(by).wait_send()
+                for place in range(N_OUTER):
+
+                    @pl.when((zz < N_Z - 1) | (place != o))
+                    def _(part=part, place=place):
+                        z_copy(part, zz, place).wait_send()
+
+            return carry
+
+        lax.fori_loop(0, N_Z, sent_z, 0)
+
+    dq_out.wait()
+    ig_out.wait()
 
 
 def shards(queries, grad_out, keys_values, inputs, kv_weight, block_order):
@@ -449,6 +469,10 @@
     hbm = pl.BlockSpec(memory_space=pl.ANY)
     dma = pltpu.SemaphoreType.DMA
     scratch = [
+        pltpu.VMEM((rows, hd), BF16),
+        pltpu.VMEM((rows, hd), BF16),
+        pltpu.VMEM((rows, hd), BF16),
+        pltpu.VMEM((tok, width // 2), BF16),
         pltpu.VMEM((4, tok, rows), F32),
         pltpu.VMEM((4, tok, rows), F32),
         pltpu.VMEM((4, 1, rows), F32),
@@ -469,14 +493,13 @@
         pltpu.VMEM((2, 2, N_Z, hd, 128), BF16),
         pltpu.VMEM((2, 3, N_Z, hd, 128), BF16),
         pltpu.VMEM((2, N_Z, hd, 128), F32),
-        pltpu.VMEM((2, N_Z - 1, hd, 128), BF16),
-        pltpu.VMEM((2, N_Z - 1, hd, 128), BF16),
-        pltpu.VMEM((N_OUTER, 32, 2 * hd), F32),
-        pltpu.VMEM((2, 32, 2 * hd), F32),
+        pltpu.VMEM((2, N_Z, 128, hd), BF16),
+        pltpu.VMEM((2, 2 * N_Z, 32, hd), BF16),
+        pltpu.VMEM((2, 32, hd), F32),
         dma((5,)), dma((5,)), dma((2, 3)), dma((2, 3)),
         dma((N_Z,)), dma((N_Z,)), dma((N_Z,)), dma, dma((2,)), dma((2,)), dma((2, 2)), dma((2, 2)),
         dma((2, 2, N_Z)), dma((2, 3, N_Z)),
-        dma((2, N_Z - 1)), dma((2, N_Z - 1)), dma((3,)), dma((2,)),
+        dma((2, N_Z, N_OUTER)), dma((2, 2 * N_Z)), pltpu.SemaphoreType.REGULAR, dma((4,)),
     ]
     query_out, input_grad, weight_grad = pl.pallas_call(
         kernel,
@@ -485,8 +508,8 @@
             jax.ShapeDtypeStruct((tok, width // 2), BF16),
             jax.ShapeDtypeStruct((64, hd), F32),
         ],
-        in_specs=[vmem, vmem, vmem, smem, hbm, hbm],
-        out_specs=[vmem, vmem, vmem],
+        in_specs=[hbm, hbm, vmem, smem, hbm, hbm],
+        out_specs=[hbm, hbm, vmem],
         scratch_shapes=scratch,
         compiler_params=pltpu.CompilerParams(
             collective_id=0, has_side_effects=True, vmem_limit_bytes=60 * 2**20

time: 66.5 us -> 63.4 us (0.953)
  Pallas kernels: 65.7 us -> 62.6 us
    pallas_call x1, Pallas kernels: 63 us -> 60 us  [shards(): pl.pallas_call(kernel, out_shape=[jax.ShapeDtypeStruct((rows, hd), BF16),...]
where the time goes in v3:
time: 63.4 us; the launch traced here: 63.2 us
  Pallas kernels  62.6 us (99%)
  between operations  0.64 us (1%)
    pallas_call x1, Pallas kernels, shards(): pl.pallas_call(kernel, out_shape=[jax.ShapeDtypeStruct((rows, hd), BF16),...  60 us
    pallas_call x1, Pallas kernels, shards(): pl.pallas_call(handover, out_shape=[jax.ShapeDtypeStruct(query_out.shape,...  2.64 us

profile of v3, /device:TPU:1, one launch (start us, length us, event | category | flops | bytes accessed | tf_op | source)
XLA Modules:
  0.0 63.2 jit_solution(841598814859460778)
XLA Ops:
  0.6 60.0 %backward.1 = (bf16[3072,128]{1,0:T(8,128)(2,1)}, bf16[384,2048]{1,0:T(8,128)(2,1)}, f32[64,128]{1,0:T(8,128)}) custom-call(bf16[3072,128]{1,0:T(8,128)(2,1)} %bitcast.11, bf16[3072,128]{1,0:T(8,128)(2,1)} %bitcast.12, bf16[768,128]{1,0:T(8,128)(2,1)} %bitcast.13, s32[128]{0:T(128)} %order.1, bf16[384,4096]{1,0:T(8,128)(2,1)} %inputs.1, ...), custom_call_target="tpu_custom_call" | custom-call | tf_op jit(solution)/shard_map/backward/pallas_call | solution.py:504
  60.6 2.6 %handover.1 = (bf16[3072,128]{1,0:T(8,128)(2,1)}, bf16[384,2048]{1,0:T(8,128)(2,1)}, f32[64,128]{1,0:T(8,128)}) custom-call(bf16[3072,128]{1,0:T(8,128)(2,1)} %get-tuple-element.9.x, bf16[384,2048]{1,0:T(8,128)(2,1)} %get-tuple-element.10.y, f32[64,128]{1,0:T(8,128)} %get-tuple-element.11.a), custom_call_target="tpu_custom_call" | custom-call | tf_op jit(solution)/shard_map/handover/pallas_call | solution.py:544

commit v4 on v3

--- a/solution.py
+++ b/solution.py
@@ -125,8 +125,8 @@
     )
     values_two = remote(kv_mid, kv.at[2, 1], kv_ss.at[3], kv_rs.at[3], inner=relay_to)
     sideways = remote(kv.at[0], kv.at[3], kv_ss.at[4], kv_rs.at[4], outer=outer(1))
-    forward = [values_mid, one, sideways, keys_two, values_two]
-    for copy in forward[:4]:
+    forward = [one, values_mid, sideways, keys_two, values_two]
+    for copy in forward[:3]:
         copy.start()
 
     def back(part, b):
@@ -198,7 +198,7 @@
             delta[:, cs] = delta[:, cs] * factor + jnp.sum(e * dp, axis=0, keepdims=True)
             return carry
 
-        lax.fori_loop(0, steps, body, 0, unroll=2)
+        lax.fori_loop(0, steps, body, 0, unroll=6)
 
     def value_step(b, n, cs):
         p = (E[b, :n, cs] * fac[b, :, cs]).astype(BF16)
@@ -214,7 +214,7 @@
             def body(t, total_so_far):
                 return total_so_far + step(b, tok, tile(t))
 
-            return lax.fori_loop(0, steps, body, jnp.zeros((tok, hd), F32), unroll=2)
+            return lax.fori_loop(0, steps, body, jnp.zeros((tok, hd), F32), unroll=6)
         parts = [None] * (tok // cut)
         for t in range(steps):
             n = (t * cut) % tok + cut
@@ -227,6 +227,7 @@
     q_in.wait()
     go_in.wait()
     look_own()
+    keys_two.start()
     values_mid.wait_recv()
     values_two.start()
     sideways.wait_recv()
@@ -396,7 +397,7 @@
         dq[cs, :] = (dot(k_t[...], ds, NN) * scale).T.astype(BF16)
         return carry
 
-    lax.fori_loop(0, steps, finish_queries, 0, unroll=2)
+    lax.fori_loop(0, steps, finish_queries, 0, unroll=3)
     dq_out.start()
     gather_y(0)
     w_local.wait()
@@ -416,7 +417,7 @@
         ig[:, cs] = term.astype(BF16)
         return carry
 
-    lax.fori_loop(0, half_d // TILE, input_part, 0, unroll=2)
+    lax.fori_loop(0, half_d // TILE, input_part, 0, unroll=4)
     ig_out.start()
     gather_z(1)
     gather_z(0)

time: 63.4 us -> 62.3 us (0.983)
  Pallas kernels: 62.6 us -> 61.4 us
    pallas_call x1, Pallas kernels: 60 us -> 58.7 us  [shards(): pl.pallas_call(kernel, out_shape=[jax.ShapeDtypeStruct((rows, hd), BF16),...]
where the time goes in v4:
time: 62.3 us; the launch traced here: 62.2 us
  Pallas kernels  61.4 us (99%)
  between operations  0.8 us (1%)
    pallas_call x1, Pallas kernels, shards(): pl.pallas_call(kernel, out_shape=[jax.ShapeDtypeStruct((rows, hd), BF16),...  58.7 us
    pallas_call x1, Pallas kernels, shards(): pl.pallas_call(handover, out_shape=[jax.ShapeDtypeStruct(query_out.shape,...  2.64 us

profile of v4, /device:TPU:1, one launch (start us, length us, event | category | flops | bytes accessed | tf_op | source)
XLA Modules:
  0.0 62.2 jit_solution(9542003625164407055)
XLA Ops:
  0.6 58.7 %backward.1 = (bf16[3072,128]{1,0:T(8,128)(2,1)}, bf16[384,2048]{1,0:T(8,128)(2,1)}, f32[64,128]{1,0:T(8,128)}) custom-call(bf16[3072,128]{1,0:T(8,128)(2,1)} %bitcast.11, bf16[3072,128]{1,0:T(8,128)(2,1)} %bitcast.12, bf16[768,128]{1,0:T(8,128)(2,1)} %bitcast.13, s32[128]{0:T(128)} %order.1, bf16[384,4096]{1,0:T(8,128)(2,1)} %inputs.1, ...), custom_call_target="tpu_custom_call" | custom-call | tf_op jit(solution)/shard_map/backward/pallas_call | solution.py:505
  59.4 2.6 %handover.1 = (bf16[3072,128]{1,0:T(8,128)(2,1)}, bf16[384,2048]{1,0:T(8,128)(2,1)}, f32[64,128]{1,0:T(8,128)}) custom-call(bf16[3072,128]{1,0:T(8,128)(2,1)} %get-tuple-element.9.x, bf16[384,2048]{1,0:T(8,128)(2,1)} %get-tuple-element.10.y, f32[64,128]{1,0:T(8,128)} %get-tuple-element.11.a), custom_call_target="tpu_custom_call" | custom-call | tf_op jit(solution)/shard_map/handover/pallas_call | solution.py:545

commit v5 on v4

--- a/solution.py
+++ b/solution.py
@@ -37,9 +37,9 @@
 
 
 def kernel(
-    q_hbm, go_hbm, kv_raw, order, inputs, weight,
+    q_hbm, go_hbm, kv_hbm, order, inputs, weight,
     dq_hbm, ig_hbm, wg,
-    q, go, dq, ig,
+    q, go, kv_raw, dq, ig,
     E, DP, top, total, delta, fac, k_t, kv, kv_mid, gout, gin, inp, w_own, w_oth, w_cat,
     pair, pair_t, ysend, yrecv, yacc, zsend, zrecv, zacc,
     kv_ss, kv_rs, g_ss, g_rs, in_ls, in_ss, in_rs, w_ls, w_ss, w_rs, p_ss, p_rs,
@@ -79,6 +79,8 @@
     two_back = inner(-2)
     relay_from = two_back // N_Y * N_Y + lax.rem(lax.rem(two_back, N_Y) + 3, N_Y)
 
+    kv_in = pltpu.make_async_copy(kv_hbm, kv_raw, io_s.at[4])
+    kv_in.start()
     barrier = pltpu.get_barrier_semaphore()
     greeted = [{"inner": inner(by)} for by in (1, 2, -1, -2)]
     greeted += [{"outer": outer(by)} for by in (1, 2, 3)]
@@ -94,6 +96,7 @@
     ig_out = pltpu.make_async_copy(ig, ig_hbm, io_s.at[3])
     q_in.start()
     go_in.start()
+    kv_in.wait()
     kv[0, 0] = kv_raw[pl.ds(0, tok, 2), :]
     kv[0, 1] = kv_raw[pl.ds(1, tok, 2), :]
     w_local = pltpu.make_async_copy(
@@ -385,8 +388,8 @@
     send_back(0, 3, block_sum(key_step, 3) * scale)
     finish_pair(0, block_sum(key_step, 0) * scale)
     pl.semaphore_wait(ready, N_Z - 1)
+    produce(0)
     gather_y(1)
-    produce(0)
 
     for b in range(4):
         k_t[:, b * tok : b * tok + tok] = kv[b, 0].astype(F32).T.astype(BF16)
@@ -472,6 +475,7 @@
     scratch = [
         pltpu.VMEM((rows, hd), BF16),
         pltpu.VMEM((rows, hd), BF16),
+        pltpu.VMEM((2 * tok, hd), BF16),
         pltpu.VMEM((rows, hd), BF16),
         pltpu.VMEM((tok, width // 2), BF16),
         pltpu.VMEM((4, tok, rows), F32),
@@ -500,7 +504,7 @@
         dma((5,)), dma((5,)), dma((2, 3)), dma((2, 3)),
         dma((N_Z,)), dma((N_Z,)), dma((N_Z,)), dma, dma((2,)), dma((2,)), dma((2, 2)), dma((2, 2)),
         dma((2, 2, N_Z)), dma((2, 3, N_Z)),
-        dma((2, N_Z, N_OUTER)), dma((2, 2 * N_Z)), pltpu.SemaphoreType.REGULAR, dma((4,)),
+        dma((2, N_Z, N_OUTER)), dma((2, 2 * N_Z)), pltpu.SemaphoreType.REGULAR, dma((5,)),
     ]
     query_out, input_grad, weight_grad = pl.pallas_call(
         kernel,
@@ -509,7 +513,7 @@
             jax.ShapeDtypeStruct((tok, width // 2), BF16),
             jax.ShapeDtypeStruct((64, hd), F32),
         ],
-        in_specs=[hbm, hbm, vmem, smem, hbm, hbm],
+        in_specs=[hbm, hbm, hbm, smem, hbm, hbm],
         out_specs=[hbm, hbm, vmem],
         scratch_shapes=scratch,
         compiler_params=pltpu.CompilerParams(

time: 62.3 us -> 62.4 us (level)
  no operation moved by 1% of the time
where the time goes in v5:
time: 62.4 us; the launch traced here: 62.2 us
  Pallas kernels  61.4 us (98%)
  between operations  0.8 us (1%)
    pallas_call x1, Pallas kernels, shards(): pl.pallas_call(kernel, out_shape=[jax.ShapeDtypeStruct((rows, hd), BF16),...  58.8 us
    pallas_call x1, Pallas kernels, shards(): pl.pallas_call(handover, out_shape=[jax.ShapeDtypeStruct(query_out.shape,...  2.64 us

profile of v5, /device:TPU:1, one launch (start us, length us, event | category | flops | bytes accessed | tf_op | source)
XLA Modules:
  0.0 62.2 jit_solution(17895584944463925430)
XLA Ops:
  0.6 58.8 %backward.1 = (bf16[3072,128]{1,0:T(8,128)(2,1)}, bf16[384,2048]{1,0:T(8,128)(2,1)}, f32[64,128]{1,0:T(8,128)}) custom-call(bf16[3072,128]{1,0:T(8,128)(2,1)} %bitcast.11, bf16[3072,128]{1,0:T(8,128)(2,1)} %bitcast.12, bf16[768,128]{1,0:T(8,128)(2,1)} %bitcast.13, s32[128]{0:T(128)} %order.1, bf16[384,4096]{1,0:T(8,128)(2,1)} %inputs.1, ...), custom_call_target="tpu_custom_call" | custom-call | tf_op jit(solution)/shard_map/backward/pallas_call | solution.py:509
  59.4 2.6 %handover.1 = (bf16[3072,128]{1,0:T(8,128)(2,1)}, bf16[384,2048]{1,0:T(8,128)(2,1)}, f32[64,128]{1,0:T(8,128)}) custom-call(bf16[3072,128]{1,0:T(8,128)(2,1)} %get-tuple-element.9.x, bf16[384,2048]{1,0:T(8,128)(2,1)} %get-tuple-element.10.y, f32[64,128]{1,0:T(8,128)} %get-tuple-element.11.a), custom_call_target="tpu_custom_call" | custom-call | tf_op jit(solution)/shard_map/handover/pallas_call | solution.py:549
